TPU v7x, 32 devices: a whole 2x2x4 slice. The times are simulated.
32 devices in a mesh: gx: 8 (over y, x, core), gy: 4 (over z).
Axes of the slice: x: 2, y: 2, z: 4, core: 2. Of those that a mesh axis runs over, the one named last changes fastest.
Arguments:
- rhs_field: float32 [64, 128, 256], P('gx', 'gy'), may hold values from -50 to 50
- alpha_coef: float32 [64, 128, 256], P('gx', 'gy'), may hold values from 0.2 to 5
- beta_coef: float32 [64, 128, 256], P('gx', 'gy'), may hold values from 0.3 to 27
Outputs:
- solution: float32 [64, 128, 256], P('gx', 'gy')
All inputs are finite; a program needn't handle non-finite values.
Results may differ from a plain program's by a relative error of at most 0.0001.
Values sent between devices are 32-bit elements; how exact they have to be, the bound alone decides.
A program may use at most 128 MiB of HBM per device.

v0:
```python
import jax
import jax.numpy as jnp
from jax import lax
from jax.sharding import PartitionSpec as P

LEVELS = 4
PRE_STEPS = 3
POST_STEPS = 3
COARSE_STEPS = 8


HELM_SHIFT = 0.05
LOW_FRACTION = 0.1


def with_halo(x, sides, width):
    for axis, dim in sides:
        peers, length = (lax.axis_size(axis), x.shape[dim])
        up = [(i, (i + 1) % peers) for i in range(peers - 1)]
        down = [(j, i) for i, j in up]
        last = lax.slice_in_dim(x, length - width, length, axis=dim)
        initial = lax.slice_in_dim(x, 0, width, axis=dim)
        before = lax.ppermute(last, axis, up)
        after = lax.ppermute(initial, axis, down)
        x = jnp.concatenate([before, x, after], axis=dim)
    return x


def restrict(values):
    first, second, third = values.shape
    return values.reshape(first // 2, 2, second // 2, 2, third // 2, 2).mean(axis=(1, 3, 5))


def prolong(values):
    return jnp.repeat(jnp.repeat(jnp.repeat(values, 2, 0), 2, 1), 2, 2)


def depth_pad(values):
    return jnp.pad(values, ((0, 0), (0, 0), (1, 1)))


def face_pad(field):
    padded = with_halo(field, (("gx", 0), ("gy", 1)), 1)
    return depth_pad(padded)


def coef_pad(beta_level):
    padded = with_halo(beta_level, (("gx", 0), ("gy", 1)), 1)
    return depth_pad(padded)


def neighbours(padded):
    return [
        padded[2:, 1:-1, 1:-1],
        padded[:-2, 1:-1, 1:-1],
        padded[1:-1, 2:, 1:-1],
        padded[1:-1, :-2, 1:-1],
        padded[1:-1, 1:-1, 2:],
        padded[1:-1, 1:-1, :-2],
    ]


def apply_op(u_padded, b_padded, alpha_level, inv_spacing):
    field = u_padded[1:-1, 1:-1, 1:-1]
    interior = b_padded[1:-1, 1:-1, 1:-1]
    summed = jnp.zeros_like(field)
    for near_u, near_b in zip(neighbours(u_padded), neighbours(b_padded)):
        summed = summed + (interior + near_b) * (field - near_u)
    return HELM_SHIFT * alpha_level * field + 0.5 * inv_spacing * summed


def smooth(field, source, alpha_level, b_padded, inv_spacing, upper, sweeps, start_zero, padder):
    lower = LOW_FRACTION * upper
    middle = 0.5 * (upper + lower)
    half_width = 0.5 * (upper - lower)
    scaled = middle / half_width
    factor = 1.0 / scaled
    if start_zero:
        residual = source
    else:
        residual = source - apply_op(padder(field), b_padded, alpha_level, inv_spacing)
    direction = residual / middle
    field = direction if start_zero else field + direction
    for k in range(1, sweeps):
        residual = source - apply_op(padder(field), b_padded, alpha_level, inv_spacing)
        factor_new = 1.0 / (2.0 * scaled - factor)
        direction = factor_new * factor * direction + 2.0 * factor_new / half_width * residual
        field = field + direction
        factor = factor_new
    return field


def descend(level_idx, sources, fields, alphas, b_pads, uppers, padder):
    inv_spacing = 1.0 / 4.0**level_idx
    smoothed = smooth(
        jnp.zeros_like(sources[level_idx]),
        sources[level_idx],
        alphas[level_idx],
        b_pads[level_idx],
        inv_spacing,
        uppers[level_idx],
        PRE_STEPS,
        True,
        padder,
    )
    residual = sources[level_idx] - apply_op(
        padder(smoothed), b_pads[level_idx], alphas[level_idx], inv_spacing
    )
    sources.append(restrict(residual))
    fields.append(smoothed)


def local(rhs_field, alpha_coef, beta_coef):
    alphas = [alpha_coef]
    betas = [beta_coef]
    for level_idx in range(1, LEVELS):
        alphas.append(restrict(alphas[-1]))
        betas.append(restrict(betas[-1]))
    maxima = jnp.stack([jnp.stack([jnp.max(alphas[i]), jnp.max(betas[i])]) for i in range(LEVELS)])
    maxima = lax.pmax(maxima, ("gx", "gy"))
    uppers = [HELM_SHIFT * maxima[i, 0] + 12.0 * maxima[i, 1] / 4.0**i for i in range(LEVELS)]
    b_pads = [coef_pad(betas[i]) for i in range(LEVELS - 2)]
    sources = [rhs_field]
    fields = []
    for level_idx in range(LEVELS - 2):
        descend(level_idx, sources, fields, alphas, b_pads, uppers, face_pad)
    second = LEVELS - 2
    last = LEVELS - 1
    coarse_inv = 1.0 / 4.0**last
    second_inv = 1.0 / 4.0**second
    b_pads.append(coef_pad(betas[second]))
    descend(second, sources, fields, alphas, b_pads, uppers, face_pad)
    coarse_beta = with_halo(betas[last], (("gx", 0), ("gy", 1)), 1)
    coarse = smooth(
        jnp.zeros_like(sources[last]),
        sources[last],
        alphas[last],
        depth_pad(coarse_beta),
        coarse_inv,
        uppers[last],
        COARSE_STEPS,
        True,
        face_pad,
    )
    smoothed = fields[second] + prolong(coarse)
    coarse = smooth(
        smoothed,
        sources[second],
        alphas[second],
        b_pads[second],
        second_inv,
        uppers[second],
        POST_STEPS,
        False,
        face_pad,
    )
    for level_idx in range(LEVELS - 3, -1, -1):
        smoothed = fields[level_idx] + prolong(coarse)
        coarse = smooth(
            smoothed,
            sources[level_idx],
            alphas[level_idx],
            b_pads[level_idx],
            1.0 / 4.0**level_idx,
            uppers[level_idx],
            POST_STEPS,
            False,
            face_pad,
        )
    return coarse


def solution(mesh):
    placed = (P("gx", "gy", None), P("gx", "gy", None), P("gx", "gy", None))
    return jax.shard_map(
        local, mesh=mesh, in_specs=placed, out_specs=P("gx", "gy", None), check_vma=False
    )
```

profile of v0, /device:TPU:28, one launch (start us, length us, event | category | flops | bytes accessed | tf_op | source)
XLA Modules:
  0.0 572.9 jit_solution(9871802513205540127)
XLA Ops:
  2.8 18.9 %reshape.134 = f32[4,2,16,2,128,2]{5,4,3,2,1,0:T(8,128)} reshape(f32[8,32,256]{2,1,0:T(8,128)} %param.5) | data formatting | bytes 524288 | tf_op jit(solution)/shard_map/reshape | solution.py:31
  21.7 7.0 %reduce_sum.103 = f32[4,16,128]{2,1,0:T(8,128)S(1)} reduce(f32[4,2,16,2,128,2]{5,4,3,2,1,0:T(8,128)} %reshape.134, f32[]{:T(128)} %constant.51.clone.1), dimensions={1,3,5}, to_apply=%region_4.0 | reduce | flops 57344 | bytes 294916 | tf_op jit(solution)/shard_map/reduce_sum | solution.py:31
  32.2 18.1 %reshape.133 = f32[4,2,16,2,128,2]{5,4,3,2,1,0:T(8,128)} reshape(f32[8,32,256]{2,1,0:T(8,128)S(1)} %copy-done.1) | data formatting | bytes 524288 | tf_op jit(solution)/shard_map/reshape | solution.py:31
  50.3 7.0 %reduce_sum.102 = f32[4,16,128]{2,1,0:T(8,128)S(1)} reduce(f32[4,2,16,2,128,2]{5,4,3,2,1,0:T(8,128)} %reshape.133, f32[]{:T(128)} %constant.51.clone.1), dimensions={1,3,5}, to_apply=%region_2.0 | reduce | flops 57344 | bytes 294916 | tf_op jit(solution)/shard_map/reduce_sum | solution.py:31
  69.0 4.5 collective-permute-start
  73.5 39.0 %pmax.7 = f32[4,2]{1,0:T(4,128)S(1)} all-reduce(f32[4,2]{1,0:T(4,128)S(1)} %pad_maximum_fusion.272), channel_id=1, replica_groups=mesh['gx'=8,'gy'=4] {'gx','gy'}, use_global_device_ids=true, to_apply=%region_16.17 | all-reduce | flops 8 | bytes 64 | tf_op jit(solution)/shard_map/pmax | solution.py:120
  123.8 4.5 collective-permute-start.5
  147.1 4.2 collective-permute-done.11
  165.8 4.5 collective-permute-start.16
  172.2 18.1 %reshape.135 = f32[4,2,16,2,128,2]{5,4,3,2,1,0:T(8,128)} reshape(f32[8,32,256]{2,1,0:T(8,128)S(1)} %fusion.65) | data formatting | bytes 524288 | tf_op jit(solution)/shard_map/reshape | solution.py:31
  190.3 7.0 %reduce_sum.112 = f32[4,16,128]{2,1,0:T(8,128)S(1)} reduce(f32[4,2,16,2,128,2]{5,4,3,2,1,0:T(8,128)} %reshape.135, f32[]{:T(128)} %constant.51.clone.1), dimensions={1,3,5}, to_apply=%region_17.18 | reduce | flops 57344 | bytes 294916 | tf_op jit(solution)/shard_map/reduce_sum | solution.py:31
  201.7 4.5 collective-permute-start.20
  207.6 4.5 collective-permute-start.21
  229.4 4.1 collective-permute-done.27
  262.2 4.5 collective-permute-start.36
  268.1 4.5 collective-permute-start.37
  290.3 4.1 collective-permute-done.43
  308.8 4.2 collective-permute-start.52
  325.6 4.3 collective-permute-start.53
  346.8 4.1 collective-permute-done.59
  362.4 4.1 collective-permute-done.63
  377.7 4.1 collective-permute-done.67
  393.0 4.1 collective-permute-done.71
  408.2 4.1 collective-permute-done.75
  439.0 4.2 collective-permute-done.83
  454.3 4.2 collective-permute-done.87
  469.6 4.2 collective-permute-done.91
  500.8 4.2 collective-permute-done.99
  516.3 4.2 collective-permute-done.103
  534.7 4.2 collective-permute-done.107
  551.0 4.2 collective-permute-done.111
  567.3 4.2 collective-permute-done.115
  (365 shorter events, 342.9 us)
Async XLA Ops:
  0.8 64.9 %collective-permute-start.2 = (f32[1,32,256]{2,1,0:T(8,128)S(1)}, f32[1,32,256]{2,1,0:T(8,128)S(1)}, u32[]{:S(2)}, u32[]{:S(2)}) collective-permute-start(f32[1,32,256]{2,1,0:T(8,128)S(1)} %get-tuple-element.86), channel_id=1, source_target_pairs={{0,4},{4,8},{8,12},{12,16},{16,20},{20,24},{24,28},{1,5},{5,9},{9,... | collective-permute-start | bytes 98312 | tf_op jit(solution)/shard_map/ppermute | solution.py:23
  69.0 49.8 %collective-permute-start = (f32[1,32,256]{2,1,0:T(8,128)S(1)}, f32[1,32,256]{2,1,0:T(8,128)S(1)}, u32[]{:S(2)}, u32[]{:S(2)}) collective-permute-start(f32[1,32,256]{2,1,0:T(8,128)S(1)} %get-tuple-element.85), channel_id=1, source_target_pairs={{4,0},{8,4},{12,8},{16,12},{20,16},{24,20},{28,24},{5,1},{9,5},{13... | collective-permute-start | bytes 98312 | tf_op jit(solution)/shard_map/ppermute | solution.py:24
  114.4 9.4 %collective-permute-start.1 = (f32[1,32,256]{2,1,0:T(8,128)S(1)}, f32[1,32,256]{2,1,0:T(8,128)S(1)}, u32[]{:S(2)}, u32[]{:S(2)}) collective-permute-start(f32[1,32,256]{2,1,0:T(8,128)S(1)} %get-tuple-element.88), channel_id=1, source_target_pairs={{4,0},{8,4},{12,8},{16,12},{20,16},{24,20},{28,24},{5,1},{9,5},{13... | collective-permute-start | bytes 98312 | tf_op jit(solution)/shard_map/ppermute | solution.py:24
  116.4 7.4 %collective-permute-start.3 = (f32[1,32,256]{2,1,0:T(8,128)S(1)}, f32[1,32,256]{2,1,0:T(8,128)S(1)}, u32[]{:S(2)}, u32[]{:S(2)}) collective-permute-start(f32[1,32,256]{2,1,0:T(8,128)S(1)} %get-tuple-element.87), channel_id=1, source_target_pairs={{0,4},{4,8},{8,12},{12,16},{16,20},{20,24},{24,28},{1,5},{5,9},{9,... | collective-permute-start | bytes 98312 | tf_op jit(solution)/shard_map/ppermute | solution.py:23
  119.0 10.7 %collective-permute-start.4 = (f32[10,1,256]{2,1,0:T(1,128)S(1)}, f32[10,1,256]{2,1,0:T(1,128)S(1)}, u32[]{:S(2)}, u32[]{:S(2)}) collective-permute-start(f32[10,1,256]{2,1,0:T(1,128)S(1)} %get-tuple-element.70), channel_id=1, source_target_pairs={{1,0},{2,1},{3,2},{5,4},{6,5},{7,6},{9,8},{10,9},{11,10},{13,12},{... | collective-permute-start | bytes 30728 | tf_op jit(solution)/shard_map/ppermute | solution.py:24
  122.5 7.2 %collective-permute-start.6 = (f32[10,1,256]{2,1,0:T(1,128)S(1)}, f32[10,1,256]{2,1,0:T(1,128)S(1)}, u32[]{:S(2)}, u32[]{:S(2)}) collective-permute-start(f32[10,1,256]{2,1,0:T(1,128)S(1)} %get-tuple-element.69), channel_id=1, source_target_pairs={{0,1},{1,2},{2,3},{4,5},{5,6},{6,7},{8,9},{9,10},{10,11},{12,13},{... | collective-permute-start | bytes 30728 | tf_op jit(solution)/shard_map/ppermute | solution.py:23
  123.8 6.2 %collective-permute-start.5 = (f32[10,1,256]{2,1,0:T(1,128)S(1)}, f32[10,1,256]{2,1,0:T(1,128)S(1)}, u32[]{:S(2)}, u32[]{:S(2)}) collective-permute-start(f32[10,1,256]{2,1,0:T(1,128)S(1)} %get-tuple-element.72), channel_id=1, source_target_pairs={{1,0},{2,1},{3,2},{5,4},{6,5},{7,6},{9,8},{10,9},{11,10},{13,12},{... | collective-permute-start | bytes 30728 | tf_op jit(solution)/shard_map/ppermute | solution.py:24
  153.9 6.3 %collective-permute-start.13 = (f32[1,32,256]{2,1,0:T(8,128)S(1)}, f32[1,32,256]{2,1,0:T(8,128)S(1)}, u32[]{:S(2)}, u32[]{:S(2)}) collective-permute-start(f32[1,32,256]{2,1,0:T(8,128)S(1)} %get-tuple-element.79), channel_id=1, source_target_pairs={{0,4},{4,8},{8,12},{12,16},{16,20},{20,24},{24,28},{1,5},{5,9},{9,... | collective-permute-start | bytes 98312 | tf_op jit(solution)/shard_map/ppermute | solution.py:23
  160.2 11.3 %collective-permute-start.14 = (f32[10,1,256]{2,1,0:T(1,128)S(1)}, f32[10,1,256]{2,1,0:T(1,128)S(1)}, u32[]{:S(2)}, u32[]{:S(2)}) collective-permute-start(f32[10,1,256]{2,1,0:T(1,128)S(1)} %get-tuple-element.66), channel_id=1, source_target_pairs={{1,0},{2,1},{3,2},{5,4},{6,5},{7,6},{9,8},{10,9},{11,10},{13,12},{... | collective-permute-start | bytes 30728 | tf_op jit(solution)/shard_map/ppermute | solution.py:24
  162.6 9.0 %collective-permute-start.15 = (f32[10,1,256]{2,1,0:T(1,128)S(1)}, f32[10,1,256]{2,1,0:T(1,128)S(1)}, u32[]{:S(2)}, u32[]{:S(2)}) collective-permute-start(f32[10,1,256]{2,1,0:T(1,128)S(1)} %get-tuple-element.65), channel_id=1, source_target_pairs={{0,1},{1,2},{2,3},{4,5},{5,6},{6,7},{8,9},{9,10},{10,11},{12,13},{... | collective-permute-start | bytes 30728 | tf_op jit(solution)/shard_map/ppermute | solution.py:23
  163.9 37.8 %collective-permute-start.18 = (f32[1,16,128]{2,1,0:T(8,128)S(1)}, f32[1,16,128]{2,1,0:T(8,128)S(1)}, u32[]{:S(2)}, u32[]{:S(2)}) collective-permute-start(f32[1,16,128]{2,1,0:T(8,128)S(1)} %get-tuple-element.114), channel_id=1, source_target_pairs={{0,4},{4,8},{8,12},{12,16},{16,20},{20,24},{24,28},{1,5},{5,9},{9,... | collective-permute-start | bytes 24584 | tf_op jit(solution)/shard_map/ppermute | solution.py:23
  165.8 35.8 %collective-permute-start.16 = (f32[1,16,128]{2,1,0:T(8,128)S(1)}, f32[1,16,128]{2,1,0:T(8,128)S(1)}, u32[]{:S(2)}, u32[]{:S(2)}) collective-permute-start(f32[1,16,128]{2,1,0:T(8,128)S(1)} %get-tuple-element.113), channel_id=1, source_target_pairs={{4,0},{8,4},{12,8},{16,12},{20,16},{24,20},{28,24},{5,1},{9,5},{13... | collective-permute-start | bytes 24584 | tf_op jit(solution)/shard_map/ppermute | solution.py:24
  197.3 10.2 %collective-permute-start.17 = (f32[1,16,128]{2,1,0:T(8,128)S(1)}, f32[1,16,128]{2,1,0:T(8,128)S(1)}, u32[]{:S(2)}, u32[]{:S(2)}) collective-permute-start(f32[1,16,128]{2,1,0:T(8,128)S(1)} %get-tuple-element.116), channel_id=1, source_target_pairs={{4,0},{8,4},{12,8},{16,12},{20,16},{24,20},{28,24},{5,1},{9,5},{13... | collective-permute-start | bytes 24584 | tf_op jit(solution)/shard_map/ppermute | solution.py:24
  199.2 8.3 %collective-permute-start.19 = (f32[1,16,128]{2,1,0:T(8,128)S(1)}, f32[1,16,128]{2,1,0:T(8,128)S(1)}, u32[]{:S(2)}, u32[]{:S(2)}) collective-permute-start(f32[1,16,128]{2,1,0:T(8,128)S(1)} %get-tuple-element.115), channel_id=1, source_target_pairs={{0,4},{4,8},{8,12},{12,16},{16,20},{20,24},{24,28},{1,5},{5,9},{9,... | collective-permute-start | bytes 24584 | tf_op jit(solution)/shard_map/ppermute | solution.py:23
  201.7 11.7 %collective-permute-start.20 = (f32[6,1,128]{2,1,0:T(1,128)S(1)}, f32[6,1,128]{2,1,0:T(1,128)S(1)}, u32[]{:S(2)}, u32[]{:S(2)}) collective-permute-start(f32[6,1,128]{2,1,0:T(1,128)S(1)} %get-tuple-element.100), channel_id=1, source_target_pairs={{1,0},{2,1},{3,2},{5,4},{6,5},{7,6},{9,8},{10,9},{11,10},{13,12},{... | collective-permute-start | bytes 9224 | tf_op jit(solution)/shard_map/ppermute | solution.py:24
  206.2 7.2 %collective-permute-start.22 = (f32[6,1,128]{2,1,0:T(1,128)S(1)}, f32[6,1,128]{2,1,0:T(1,128)S(1)}, u32[]{:S(2)}, u32[]{:S(2)}) collective-permute-start(f32[6,1,128]{2,1,0:T(1,128)S(1)} %get-tuple-element.99), channel_id=1, source_target_pairs={{0,1},{1,2},{2,3},{4,5},{5,6},{6,7},{8,9},{9,10},{10,11},{12,13},{... | collective-permute-start | bytes 9224 | tf_op jit(solution)/shard_map/ppermute | solution.py:23
  207.6 6.2 %collective-permute-start.21 = (f32[6,1,128]{2,1,0:T(1,128)S(1)}, f32[6,1,128]{2,1,0:T(1,128)S(1)}, u32[]{:S(2)}, u32[]{:S(2)}) collective-permute-start(f32[6,1,128]{2,1,0:T(1,128)S(1)} %get-tuple-element.102), channel_id=1, source_target_pairs={{1,0},{2,1},{3,2},{5,4},{6,5},{7,6},{9,8},{10,9},{11,10},{13,12},{... | collective-permute-start | bytes 9224 | tf_op jit(solution)/shard_map/ppermute | solution.py:24
  241.6 9.1 %collective-permute-start.30 = (f32[6,1,128]{2,1,0:T(1,128)S(1)}, f32[6,1,128]{2,1,0:T(1,128)S(1)}, u32[]{:S(2)}, u32[]{:S(2)}) collective-permute-start(f32[6,1,128]{2,1,0:T(1,128)S(1)} %get-tuple-element.96), channel_id=1, source_target_pairs={{1,0},{2,1},{3,2},{5,4},{6,5},{7,6},{9,8},{10,9},{11,10},{13,12},{... | collective-permute-start | bytes 9224 | tf_op jit(solution)/shard_map/ppermute | solution.py:24
  243.8 6.9 %collective-permute-start.31 = (f32[6,1,128]{2,1,0:T(1,128)S(1)}, f32[6,1,128]{2,1,0:T(1,128)S(1)}, u32[]{:S(2)}, u32[]{:S(2)}) collective-permute-start(f32[6,1,128]{2,1,0:T(1,128)S(1)} %get-tuple-element.95), channel_id=1, source_target_pairs={{0,1},{1,2},{2,3},{4,5},{5,6},{6,7},{8,9},{9,10},{10,11},{12,13},{... | collective-permute-start | bytes 9224 | tf_op jit(solution)/shard_map/ppermute | solution.py:23
  245.1 17.1 %collective-permute-start.32 = (f32[1,8,64]{2,1,0:T(8,128)S(1)}, f32[1,8,64]{2,1,0:T(8,128)S(1)}, u32[]{:S(2)}, u32[]{:S(2)}) collective-permute-start(f32[1,8,64]{2,1,0:T(8,128)S(1)} %get-tuple-element.146), channel_id=1, source_target_pairs={{4,0},{8,4},{12,8},{16,12},{20,16},{24,20},{28,24},{5,1},{9,5},{13... | collective-permute-start | bytes 6152 | tf_op jit(solution)/shard_map/ppermute | solution.py:24
  247.0 15.2 %collective-permute-start.34 = (f32[1,8,64]{2,1,0:T(8,128)S(1)}, f32[1,8,64]{2,1,0:T(8,128)S(1)}, u32[]{:S(2)}, u32[]{:S(2)}) collective-permute-start(f32[1,8,64]{2,1,0:T(8,128)S(1)} %get-tuple-element.145), channel_id=1, source_target_pairs={{0,4},{4,8},{8,12},{12,16},{16,20},{20,24},{24,28},{1,5},{5,9},{9,... | collective-permute-start | bytes 6152 | tf_op jit(solution)/shard_map/ppermute | solution.py:23
  256.2 11.9 %collective-permute-start.33 = (f32[1,8,64]{2,1,0:T(8,128)S(1)}, f32[1,8,64]{2,1,0:T(8,128)S(1)}, u32[]{:S(2)}, u32[]{:S(2)}) collective-permute-start(f32[1,8,64]{2,1,0:T(8,128)S(1)} %get-tuple-element.149), channel_id=1, source_target_pairs={{4,0},{8,4},{12,8},{16,12},{20,16},{24,20},{28,24},{5,1},{9,5},{13... | collective-permute-start | bytes 6152 | tf_op jit(solution)/shard_map/ppermute | solution.py:24
  260.2 7.8 %collective-permute-start.35 = (f32[1,8,64]{2,1,0:T(8,128)S(1)}, f32[1,8,64]{2,1,0:T(8,128)S(1)}, u32[]{:S(2)}, u32[]{:S(2)}) collective-permute-start(f32[1,8,64]{2,1,0:T(8,128)S(1)} %get-tuple-element.148), channel_id=1, source_target_pairs={{0,4},{4,8},{8,12},{12,16},{16,20},{20,24},{24,28},{1,5},{5,9},{9,... | collective-permute-start | bytes 6152 | tf_op jit(solution)/shard_map/ppermute | solution.py:23
  262.2 11.7 %collective-permute-start.36 = (f32[4,1,64]{2,1,0:T(1,128)S(1)}, f32[4,1,64]{2,1,0:T(1,128)S(1)}, u32[]{:S(2)}, u32[]{:S(2)}) collective-permute-start(f32[4,1,64]{2,1,0:T(1,128)S(1)} %get-tuple-element.132), channel_id=1, source_target_pairs={{1,0},{2,1},{3,2},{5,4},{6,5},{7,6},{9,8},{10,9},{11,10},{13,12},{... | collective-permute-start | bytes 3080 | tf_op jit(solution)/shard_map/ppermute | solution.py:24
  266.7 7.2 %collective-permute-start.38 = (f32[4,1,64]{2,1,0:T(1,128)S(1)}, f32[4,1,64]{2,1,0:T(1,128)S(1)}, u32[]{:S(2)}, u32[]{:S(2)}) collective-permute-start(f32[4,1,64]{2,1,0:T(1,128)S(1)} %get-tuple-element.131), channel_id=1, source_target_pairs={{0,1},{1,2},{2,3},{4,5},{5,6},{6,7},{8,9},{9,10},{10,11},{12,13},{... | collective-permute-start | bytes 3080 | tf_op jit(solution)/shard_map/ppermute | solution.py:23
  294.6 10.3 %collective-permute-start.44 = (f32[1,8,64]{2,1,0:T(8,128)S(1)}, f32[1,8,64]{2,1,0:T(8,128)S(1)}, u32[]{:S(2)}, u32[]{:S(2)}) collective-permute-start(f32[1,8,64]{2,1,0:T(8,128)S(1)} %get-tuple-element.142), channel_id=1, source_target_pairs={{4,0},{8,4},{12,8},{16,12},{20,16},{24,20},{28,24},{5,1},{9,5},{13... | collective-permute-start | bytes 6152 | tf_op jit(solution)/shard_map/ppermute | solution.py:24
  296.5 8.4 %collective-permute-start.45 = (f32[1,8,64]{2,1,0:T(8,128)S(1)}, f32[1,8,64]{2,1,0:T(8,128)S(1)}, u32[]{:S(2)}, u32[]{:S(2)}) collective-permute-start(f32[1,8,64]{2,1,0:T(8,128)S(1)} %get-tuple-element.141), channel_id=1, source_target_pairs={{0,4},{4,8},{8,12},{12,16},{16,20},{20,24},{24,28},{1,5},{5,9},{9,... | collective-permute-start | bytes 6152 | tf_op jit(solution)/shard_map/ppermute | solution.py:23
  298.9 9.5 %collective-permute-start.48 = (f32[1,4,32]{2,1,0:T(4,128)S(1)}, f32[1,4,32]{2,1,0:T(4,128)S(1)}, u32[]{:S(2)}, u32[]{:S(2)}) collective-permute-start(f32[1,4,32]{2,1,0:T(4,128)S(1)} %get-tuple-element.166), channel_id=1, source_target_pairs={{4,0},{8,4},{12,8},{16,12},{20,16},{24,20},{28,24},{5,1},{9,5},{13... | collective-permute-start | bytes 1544 | tf_op jit(solution)/shard_map/ppermute | solution.py:24
  304.9 10.7 %collective-permute-start.46 = (f32[4,1,64]{2,1,0:T(1,128)S(1)}, f32[4,1,64]{2,1,0:T(1,128)S(1)}, u32[]{:S(2)}, u32[]{:S(2)}) collective-permute-start(f32[4,1,64]{2,1,0:T(1,128)S(1)} %get-tuple-element.128), channel_id=1, source_target_pairs={{1,0},{2,1},{3,2},{5,4},{6,5},{7,6},{9,8},{10,9},{11,10},{13,12},{... | collective-permute-start | bytes 3080 | tf_op jit(solution)/shard_map/ppermute | solution.py:24
  307.1 8.5 %collective-permute-start.47 = (f32[4,1,64]{2,1,0:T(1,128)S(1)}, f32[4,1,64]{2,1,0:T(1,128)S(1)}, u32[]{:S(2)}, u32[]{:S(2)}) collective-permute-start(f32[4,1,64]{2,1,0:T(1,128)S(1)} %get-tuple-element.127), channel_id=1, source_target_pairs={{0,1},{1,2},{2,3},{4,5},{5,6},{6,7},{8,9},{9,10},{10,11},{12,13},{... | collective-permute-start | bytes 3080 | tf_op jit(solution)/shard_map/ppermute | solution.py:23
  308.8 12.9 %collective-permute-start.52 = (f32[3,1,32]{2,1,0:T(1,128)S(1)}, f32[3,1,32]{2,1,0:T(1,128)S(1)}, u32[]{:S(2)}, u32[]{:S(2)}) collective-permute-start(f32[3,1,32]{2,1,0:T(1,128)S(1)} %get-tuple-element.163), channel_id=1, source_target_pairs={{1,0},{2,1},{3,2},{5,4},{6,5},{7,6},{9,8},{10,9},{11,10},{13,12},{... | collective-permute-start | bytes 1160 | tf_op jit(solution)/shard_map/ppermute | solution.py:24
  313.0 8.7 %collective-permute-start.54 = (f32[3,1,32]{2,1,0:T(1,128)S(1)}, f32[3,1,32]{2,1,0:T(1,128)S(1)}, u32[]{:S(2)}, u32[]{:S(2)}) collective-permute-start(f32[3,1,32]{2,1,0:T(1,128)S(1)} %get-tuple-element.162), channel_id=1, source_target_pairs={{0,1},{1,2},{2,3},{4,5},{5,6},{6,7},{8,9},{9,10},{10,11},{12,13},{... | collective-permute-start | bytes 1160 | tf_op jit(solution)/shard_map/ppermute | solution.py:23
  (87 other events, 557.4 us)
where the time goes:
time: 577 us; the launch traced here: 573 us
  starting transfers between devices  250 us (43%)
  waiting for transfers between devices  165 us (29%)
  local copies, waits for them, and re-layouts  67.5 us (12%)
  other arithmetic  43.1 us (7%)
  blocking collectives  39 us (7%)
  between operations  8.44 us (1%)
    ppermute x58, waiting for transfers between devices, with_halo(): before = lax.ppermute(last, axis, up)  164 us
    ppermute x58, starting transfers between devices, with_halo(): after = lax.ppermute(initial, axis, down)  146 us
    ppermute x58, starting transfers between devices, with_halo(): before = lax.ppermute(last, axis, up)  104 us
    reshape x4, local copies, waits for them, and re-layouts, restrict(): values.reshape(first // 2, 2, second // 2, 2, third // 2, 2)  58.5 us
    pmax x1, blocking collectives, local(): maxima = lax.pmax(maxima, ('gx', 'gy'))  39 us
    reduce_sum x10, other arithmetic, restrict(): values.reshape(first // 2, 2, second // 2, 2, third // 2, 2)  23.6 us
  transfers between devices with their start and end apart: 116, of which 47 were waited for; matrix products, arithmetic and copies ran while one was open for 17% of the time, Pallas kernels for 0%

commit v1 on v0

v1 whole, which is shorter than its diff:
```python
import functools

import jax
import jax.numpy as jnp
from jax import lax
from jax.experimental import pallas as pl
from jax.experimental.pallas import tpu as pltpu
from jax.sharding import PartitionSpec as P

PRE_STEPS = 3
POST_STEPS = 3
COARSE_STEPS = 8
HELM_SHIFT = 0.05
LOW_FRACTION = 0.1
LANES = 128
HALO = 3
MESH = pl.DeviceIdType.MESH
DIRS = [(1, 0), (-1, 0), (0, 1), (0, -1), (1, 1), (1, -1), (-1, 1), (-1, -1)]
HIGH = lax.Precision.HIGHEST


def dot(a, b):
    return jnp.dot(a, b, precision=HIGH, preferred_element_type=jnp.float32)


def iota(shape, dim):
    return lax.broadcasted_iota(jnp.int32, shape, dim)


def pick(rows, cols, cond):
    return cond(iota((rows, cols), 0), iota((rows, cols), 1)).astype(jnp.float32)


def roll(x, shift, axis):
    return pltpu.roll(x, shift % x.shape[axis], axis)


def restrict_sum(values, out_lanes):
    planes, rows, lanes = values.shape
    pairs = values.reshape(planes // 2, 2, rows, lanes)
    summed = (pairs[:, 0] + pairs[:, 1]).reshape(planes // 2 * rows, lanes)
    narrow = dot(summed, pick(lanes, out_lanes, lambda i, j: (i >> 1) == j))
    total = planes // 2 * rows
    small = dot(pick(total // 2, total, lambda i, j: (j >> 1) == i), narrow)
    return (0.125 * small).reshape(planes // 2, rows // 2, out_lanes)


class Exchange:
    def __init__(self, buf, st_next, st_prev, sems, slot, x_len, y_len, place, peers):
        self.buf, self.st_next, self.st_prev = buf, st_next, st_prev
        self.send, self.recv = sems
        self.slot, self.x_len, self.y_len = slot, x_len, y_len
        self.place, self.peers = place, peers

    def region(self, dx, dy):
        x_len, y_len = self.x_len, self.y_len
        if dx == 0:
            src_x = dst_x = pl.ds(HALO, x_len)
        elif dx == 1:
            src_x, dst_x = pl.ds(x_len, HALO), pl.ds(0, HALO)
        else:
            src_x, dst_x = pl.ds(HALO, HALO), pl.ds(x_len + HALO, HALO)
        if dy == 0:
            return (self.buf.at[:, src_x, pl.ds(0, y_len)],
                    self.buf.at[:, dst_x, pl.ds(0, y_len)])
        if dy == 1:
            return self.buf.at[:, src_x, pl.ds(y_len - 8, 8)], self.st_prev.at[:, dst_x]
        return self.buf.at[:, src_x, pl.ds(0, 8)], self.st_next.at[:, dst_x]

    def inside(self, dx, dy):
        x, y = self.place[0] + dx, self.place[1] + dy
        return (x >= 0) & (x < self.peers[0]) & (y >= 0) & (y < self.peers[1])

    def copy(self, k):
        dx, dy = DIRS[k]
        src, dst = self.region(dx, dy)
        return pltpu.make_async_remote_copy(
            src_ref=src, dst_ref=dst,
            send_sem=self.send.at[self.slot, k], recv_sem=self.recv.at[self.slot, k],
            device_id=(self.place[0] + dx, self.place[1] + dy), device_id_type=MESH)

    def clear(self):
        for dx, dy in DIRS:
            @pl.when(jnp.logical_not(self.inside(-dx, -dy)))
            def _():
                _, dst = self.region(dx, dy)
                dst[...] = jnp.zeros(dst.shape, jnp.float32)

    def start(self):
        for k, (dx, dy) in enumerate(DIRS):
            @pl.when(self.inside(dx, dy))
            def _():
                self.copy(k).start()

    def finish(self):
        for k, (dx, dy) in enumerate(DIRS):
            @pl.when(self.inside(dx, dy))
            def _():
                self.copy(k).wait_send()

            @pl.when(self.inside(-dx, -dy))
            def _():
                self.copy(k).wait_recv()
        shape = self.st_next.shape
        near = iota(shape, 2) < 4
        self.buf[:, :, pl.ds(self.y_len, 8)] = jnp.where(near, self.st_next[...], self.st_prev[...])


def over(start, count, chunk, body):
    if count == chunk:
        body(start)
        return

    def step(i, carry):
        body(start + i * chunk)
        return carry

    lax.fori_loop(0, count // chunk, step, 0)


def build(level, start, count, chunk, alpha_at, beta_at, z_len, wrap_y, coefs):
    dia, c_x, c_y, c_z = coefs
    h = 0.5 / 4.0**level

    def body(i):
        b = beta_at(i)
        up, down = beta_at(i + 1), beta_at(i - 1)
        shape = b.shape
        lane, row = iota(shape, 2), iota(shape, 1)
        y_up, y_down = roll(b, -1, 1), roll(b, 1, 1)
        if not wrap_y:
            y_up = jnp.where(row == shape[1] - 1, 0.0, y_up)
            y_down = jnp.where(row == 0, 0.0, y_down)
        z_up = jnp.where(lane == z_len - 1, 0.0, roll(b, -1, 2))
        z_down = jnp.where(lane == 0, 0.0, roll(b, 1, 2))
        total = 6.0 * b + (up + down) + (y_up + y_down) + (z_up + z_down)
        dia[pl.ds(i, chunk)] = HELM_SHIFT * alpha_at(i) + h * total
        for out, near in ((c_x, up), (c_y, y_up), (c_z, z_up)):
            out[pl.ds(i, chunk)] = jnp.where(jnp.minimum(b, near) > 0.0, h * (b + near), 0.0)

    over(start, count, chunk, body)


def apply_op(coefs, u, i, chunk):
    dia, c_x, c_y, c_z = coefs
    here = pl.ds(i, chunk)
    mid = u[here]
    y_c, z_c = c_y[here], c_z[here]
    off = c_x[here] * u[pl.ds(i + 1, chunk)] + c_x[pl.ds(i - 1, chunk)] * u[pl.ds(i - 1, chunk)]
    off += y_c * roll(mid, -1, 1) + roll(y_c * mid, 1, 1)
    off += z_c * roll(mid, -1, 2) + roll(z_c * mid, 1, 2)
    return mid, dia[here] * mid - off


def cheb(upper, steps):
    lower = LOW_FRACTION * upper
    middle, half = 0.5 * (upper + lower), 0.5 * (upper - lower)
    scaled = middle / half
    factor = 1.0 / scaled
    out = [(None, 1.0 / middle)]
    for _ in range(1, steps):
        new = 1.0 / (2.0 * scaled - factor)
        out.append((new * factor, 2.0 * new / half))
        factor = new
    return out


def sweep(coefs, u, u_new, d, f_at, a, b, start, count, chunk):
    def body(i):
        mid, au = apply_op(coefs, u, i, chunk)
        step = b * (f_at(i) - au)
        if a is not None:
            step += a * d[pl.ds(i, chunk)]
        d[pl.ds(i, chunk)] = step
        u_new[pl.ds(i, chunk)] = mid + step

    over(start, count, chunk, body)


def first(u, d, f_at, b, start, count, chunk):
    def body(i):
        step = b * f_at(i)
        d[pl.ds(i, chunk)] = step
        u[pl.ds(i, chunk)] = step

    over(start, count, chunk, body)


def residual(coefs, u, f_at, res, start, count, chunk):
    def body(i):
        _, au = apply_op(coefs, u, i, chunk)
        res[pl.ds(i - start, chunk)] = f_at(i) - au

    over(start, count, chunk, body)


def planes_at(ref, lead, chunk):
    if lead is None:
        return lambda i: ref[pl.ds(i, chunk)]
    return lambda i: ref[lead, pl.ds(i, chunk)]


def kernel(peers, dims, rhs, alpha, beta, out, sc):
    n_x, n_y = peers
    n = n_x * n_y
    g_x, g_y = lax.axis_index("gx"), lax.axis_index("gy")
    place = (g_x, g_y)
    me = g_x * n_y + g_y
    (x0, y0, z0), (x1, y1, z1), (x2, y2, z2), (x3, y3, z3) = dims
    X2, Y2, X3, Y3 = n_x * x2, n_y * y2, n_x * x3, n_y * y3
    sems = (sc["halo_send"], sc["halo_recv"])

    barrier = pltpu.get_barrier_semaphore()

    def greet(t, carry):
        j = lax.rem(me + t, n)
        pl.semaphore_signal(barrier, inc=1, device_id=(lax.div(j, n_y), lax.rem(j, n_y)),
                            device_id_type=MESH)
        return carry

    lax.fori_loop(1, n, greet, 0)

    def exchange(name, slot, x_len, y_len):
        return Exchange(sc[name], sc[name + "_n"], sc[name + "_p"], sems, slot, x_len, y_len,
                        place, peers)

    ex_in = exchange("in0", 0, x0, y0)
    ex_ab = exchange("ab1", 1, x1, y1)
    ex_f1 = exchange("f1", 2, x1, y1)
    ex_u0 = exchange("u0", 3, x0, y0)
    ex_u1 = exchange("u1", 4, x1, y1)
    ex_v1 = exchange("v1", 5, x1, y1)

    def gather_start(slot, src, dst_of, junk):
        send, recv = sc["all_send"].at[slot], sc["all_recv"].at[slot]

        def one(t, carry):
            j = lax.rem(me + t, n)
            pltpu.make_async_remote_copy(
                src_ref=src, dst_ref=dst_of(), send_sem=send, recv_sem=recv,
                device_id=(lax.div(j, n_y), lax.rem(j, n_y)), device_id_type=MESH).start()
            return carry

        lax.fori_loop(1, n, one, 0)
        pltpu.make_async_copy(src, dst_of(), recv).start()
        pltpu.make_async_copy(src, junk, send).start()

    def gather_wait(slot, whole):
        pltpu.make_async_copy(whole, whole, sc["all_recv"].at[slot]).wait()
        pltpu.make_async_copy(whole, whole, sc["all_send"].at[slot]).wait()

    def mine(ref):
        return ref.at[pl.ds(g_x * x2, x2), pl.ds(pl.multiple_of(g_y * y2, y2), y2)]

    in0 = sc["in0"]
    for k, ref in enumerate((rhs, alpha, beta)):
        in0[k, pl.ds(HALO, x0), pl.ds(0, y0)] = ref[...]
    pl.semaphore_wait(barrier, n - 1)
    ex_in.start()

    a1, b1 = restrict_sum(alpha[...], LANES), restrict_sum(beta[...], LANES)
    row = iota((8, LANES), 0)
    tile = jnp.where(row == 0, jnp.max(alpha[...]), 0.0)
    for k, value in ((1, jnp.max(beta[...])), (2, jnp.max(a1)), (3, jnp.max(b1))):
        tile = jnp.where(row == k, value, tile)
    sc["top"][...] = tile
    gather_start(0, sc["top"], lambda: sc["tops"].at[me], sc["top_junk"])
    ab1 = sc["ab1"]
    ab1[0, pl.ds(HALO, x1), pl.ds(0, y1)] = a1
    ab1[1, pl.ds(HALO, x1), pl.ds(0, y1)] = b1
    ex_ab.start()
    sc["ab2_src"][...] = restrict_sum(a1, LANES) + roll(restrict_sum(b1, LANES), z2, 2)
    gather_start(1, sc["ab2_src"], lambda: mine(sc["ab2"]), sc["ab2_junk"])

    for ex in (ex_in, ex_ab, ex_f1, ex_u0, ex_u1, ex_v1):
        ex.clear()

    ex_in.finish()
    k0 = [sc[k] for k in ("dia0", "cx0", "cy0", "cz0")]
    lo = HALO
    build(0, 1, x0 + 4, 1, planes_at(in0, 1, 1), planes_at(in0, 2, 1), z0, True, k0)
    sc["cx0"][0:1] = jnp.where(jnp.minimum(in0[2, 0:1], in0[2, 1:2]) > 0.0,
                               0.5 * (in0[2, 0:1] + in0[2, 1:2]), 0.0)
    gather_wait(0, sc["tops"])
    tops = jnp.max(sc["tops"][...], axis=0)
    wide = jnp.concatenate([tops, tops], axis=1)
    upper0 = HELM_SHIFT * wide[0:1] + 12.0 * wide[1:2]
    upper1 = HELM_SHIFT * tops[2:3] + 12.0 * tops[3:4] / 4.0
    ch0 = cheb(upper0, PRE_STEPS)
    ch1 = cheb(upper1, PRE_STEPS)
    f0 = planes_at(in0, 0, 1)
    ua, ub, d0 = sc["ua0"], sc["ub0"], sc["d0"]
    first(ua, d0, f0, ch0[0][1], 0, x0 + 6, 1)
    sweep(k0, ua, ub, d0, f0, *ch0[1], 1, x0 + 4, 1)
    sweep(k0, ub, ua, d0, f0, *ch0[2], 2, x0 + 2, 1)
    sc["u0"][0, pl.ds(lo, x0), pl.ds(0, y0)] = ua[pl.ds(lo, x0), pl.ds(0, y0)]
    residual(k0, ua, f0, sc["r0"], lo, x0, 1)
    sc["f1"][0, pl.ds(HALO, x1), pl.ds(0, y1)] = restrict_sum(sc["r0"][:, 0:y0], LANES)
    ex_f1.start()
    ex_u0.start()

    ex_ab.finish()
    k1 = [sc[k] for k in ("dia1", "cx1", "cy1", "cz1")]
    build(1, 1, x1 + 4, 2, planes_at(ab1, 0, 2), planes_at(ab1, 1, 2), z1, True, k1)
    sc["cx1"][0:1] = jnp.where(jnp.minimum(ab1[1, 0:1], ab1[1, 1:2]) > 0.0,
                               0.125 * (ab1[1, 0:1] + ab1[1, 1:2]), 0.0)
    ex_f1.finish()
    f1 = planes_at(sc["f1"], 0, 2)
    ua1, ub1, d1 = sc["ua1"], sc["ub1"], sc["d1"]
    first(ua1, d1, f1, ch1[0][1], 0, x1 + 6, 2)
    sweep(k1, ua1, ub1, d1, f1, *ch1[1], 1, x1 + 4, 2)
    sweep(k1, ub1, ua1, d1, f1, *ch1[2], 2, x1 + 2, 2)
    residual(k1, ua1, f1, sc["r1"], HALO, x1, 2)
    sc["f2_src"][...] = restrict_sum(sc["r1"][:, 0:y1], LANES)
    gather_start(2, sc["f2_src"], lambda: mine(sc["f2"]), sc["f2_junk"])
    sc["u1"][0, pl.ds(HALO, x1), pl.ds(0, y1)] = ua1[pl.ds(HALO, x1), pl.ds(0, y1)]
    ex_u1.start()

    k2 = [sc[k] for k in ("dia2", "cx2", "cy2", "cz2")]
    k3 = [sc[k] for k in ("dia3", "cx3", "cy3", "cz3")]
    ua2, ub2, d2 = sc["ua2"], sc["ub2"], sc["d2"]
    ua3, ub3, d3, f3 = sc["ua3"], sc["ub3"], sc["d3"], sc["f3"]
    for ref, size in ((ua2, X2), (ub2, X2), (sc["cx2"], X2), (d2, X2),
                      (ua3, X3), (ub3, X3), (sc["cx3"], X3), (d3, X3)):
        for at in (0, size + 1):
            ref[at] = jnp.zeros(ref.shape[1:], jnp.float32)
    gather_wait(1, sc["ab2"])
    q2 = 2 if X2 % 2 == 0 else 1
    q3 = X3 if X3 * Y3 <= 256 else 1
    fine = max(1, 256 // Y2) * 2
    fine = min(fine, X2)

    def unpack(i):
        both = sc["ab2"][pl.ds(i, q2)]
        lane = iota(both.shape, 2)
        ub2[pl.ds(i + 1, q2)] = jnp.where(lane < z2, both, 0.0)
        d2[pl.ds(i + 1, q2)] = jnp.where(lane < z2, roll(both, z2, 2), 0.0)

    over(0, X2, q2, unpack)

    def shrink(i):
        at, to = i * fine, i * (fine // 2)
        ub3[pl.ds(to + 1, fine // 2)] = restrict_sum(ub2[pl.ds(at + 1, fine)], LANES)
        d3[pl.ds(to + 1, fine // 2)] = restrict_sum(d2[pl.ds(at + 1, fine)], LANES)

    over(0, X2 // fine, 1, shrink)
    build(2, 1, X2, q2, planes_at(ub2, None, q2), planes_at(d2, None, q2), z2, False, k2)
    build(3, 1, X3, q3, planes_at(ub3, None, q3), planes_at(d3, None, q3), z3, False, k3)

    def largest(ref):
        best = jnp.max(jnp.max(ref[...], axis=0), axis=0, keepdims=True)
        return jnp.max(best, axis=1, keepdims=True) + jnp.zeros((1, LANES), jnp.float32)

    ch2 = cheb(HELM_SHIFT * largest(ub2) + 12.0 * largest(d2) / 16.0, PRE_STEPS)
    ch3 = cheb(HELM_SHIFT * largest(ub3) + 12.0 * largest(d3) / 64.0, COARSE_STEPS)
    gather_wait(2, sc["f2"])
    f2 = lambda i: sc["f2"][pl.ds(i - 1, q2)]
    first(ua2, d2, f2, ch2[0][1], 1, X2, q2)
    sweep(k2, ua2, ub2, d2, f2, *ch2[1], 1, X2, q2)
    sweep(k2, ub2, ua2, d2, f2, *ch2[2], 1, X2, q2)
    residual(k2, ua2, f2, ub2, 1, X2, q2)

    def shrink_f(i):
        at, to = i * fine, i * (fine // 2)
        f3[pl.ds(to + 1, fine // 2)] = restrict_sum(ub2[pl.ds(at, fine)], LANES)

    over(0, X2 // fine, 1, shrink_f)
    f3_at = planes_at(f3, None, q3)
    first(ua3, d3, f3_at, ch3[0][1], 1, X3, q3)
    now, later = ua3, ub3
    for a, b in ch3[1:]:
        sweep(k3, now, later, d3, f3_at, a, b, 1, X3, q3)
        now, later = later, now
    widen = pick(LANES, LANES, lambda i, j: (j >> 1) == i)
    part = max(1, fine // 2)
    rows3 = part * Y3

    def grow(i):
        small = dot(now[pl.ds(i * part + 1, part)].reshape(rows3, LANES), widen)
        tall = dot(pick(2 * rows3, rows3, lambda r, c: (r >> 1) == c), small)
        tall = tall.reshape(part, Y2, LANES)
        at = i * (2 * part) + 1
        lane = iota((Y2, LANES), 1)
        for k in range(part):
            add = jnp.where(lane < z2, tall[k], 0.0)
            ua2[at + 2 * k] = ua2[at + 2 * k] + add
            ua2[at + 2 * k + 1] = ua2[at + 2 * k + 1] + add

    over(0, X3 // part, 1, grow)
    ub2[0] = jnp.zeros(ub2.shape[1:], jnp.float32)
    ub2[X2 + 1] = jnp.zeros(ub2.shape[1:], jnp.float32)
    sweep(k2, ua2, ub2, d2, f2, None, ch2[0][1], 1, X2, q2)
    sweep(k2, ub2, ua2, d2, f2, *ch2[1], 1, X2, q2)
    sweep(k2, ua2, ub2, d2, f2, *ch2[2], 1, X2, q2)

    ex_u1.finish()
    here = pl.multiple_of(g_y * y2, 8)
    before = pl.multiple_of(jnp.maximum(g_y * y2 - 8, 0), 8)
    after = pl.multiple_of(jnp.minimum(g_y * y2 + y2, Y2 - 8), 8)
    turn = pick(y1 + 8, y2 + 16,
                lambda r, c: c == jnp.where(r < y1 + 4, 8 + (r >> 1), 6 + ((r - y1 - 4) >> 1)))
    u1 = sc["u1"]
    for k in range(x2 + 4):
        at = jnp.clip(g_x * x2 - 2 + k, 0, X2 - 1) + 1
        block = jnp.concatenate([ub2[at, pl.ds(before, 8)], ub2[at, pl.ds(here, y2)],
                                 ub2[at, pl.ds(after, 8)]], axis=0)
        block = dot(turn, dot(block, widen))
        for to in (2 * k - 1, 2 * k):
            if 0 <= to < x1 + 6:
                ua1[to] = u1[0, to] + block
    sweep(k1, ua1, ub1, d1, f1, None, ch1[0][1], 1, x1 + 4, 2)
    sweep(k1, ub1, ua1, d1, f1, *ch1[1], 2, x1 + 2, 2)
    sweep(k1, ua1, ub1, d1, f1, *ch1[2], 3, x1, 2)
    sc["v1"][0, pl.ds(HALO, x1), pl.ds(0, y1)] = ub1[pl.ds(HALO, x1), pl.ds(0, y1)]
    ex_v1.start()

    ex_u0.finish()
    ex_v1.finish()
    v1, u0 = sc["v1"], sc["u0"]
    widen0 = pick(z1, z0, lambda i, j: (j >> 1) == i)
    turn0 = pick(y0 + 8, y1 + 8,
                 lambda r, c: c == jnp.where(r < y0 + 4, r >> 1, y1 + 6 + ((r - y0 - 4) >> 1)))
    for k in range(x1 + 4):
        block = dot(dot(turn0, v1[0, k + 1]), widen0)
        for to in (2 * k - 1, 2 * k):
            if 0 <= to < x0 + 6:
                ua[to] = u0[0, to] + block
    sweep(k0, ua, ub, d0, f0, None, ch0[0][1], 1, x0 + 4, 1)
    sweep(k0, ub, ua, d0, f0, *ch0[1], 2, x0 + 2, 1)

    def last(i):
        mid, au = apply_op(k0, ua, i, 1)
        a, b = ch0[2]
        value = mid + (a * d0[pl.ds(i, 1)] + b * (f0(i) - au))
        out[pl.ds(i - lo, 1)] = value[:, 0:y0]

    over(lo, x0, 1, last)


def local(peers, rhs_field, alpha_coef, beta_coef):
    n_x, n_y = peers
    n = n_x * n_y
    x0, y0, z0 = rhs_field.shape
    dims = [(x0 >> k, y0 >> k, z0 >> k) for k in range(4)]
    (x0, y0, z0), (x1, y1, z1), (x2, y2, z2), (x3, y3, z3) = dims
    X2, Y2, X3, Y3 = n_x * x2, n_y * y2, n_x * x3, n_y * y3
    wide = {"in0": (3, x0, y0, z0), "ab1": (2, x1, y1, z1), "f1": (1, x1, y1, z1),
            "u0": (1, x0, y0, z0), "u1": (1, x1, y1, z1), "v1": (1, x1, y1, z1)}
    shapes = {}
    for name, (k, x, y, z) in wide.items():
        shapes[name] = (k, x + 2 * HALO, y + 8, z)
        shapes[name + "_n"] = shapes[name + "_p"] = (k, x + 2 * HALO, 8, z)
    full0, full1 = (x0 + 6, y0 + 8, z0), (x1 + 6, y1 + 8, z1)
    full2, full3 = (X2 + 2, Y2, LANES), (X3 + 2, Y3, LANES)
    for name, full in (("0", full0), ("1", full1), ("2", full2), ("3", full3)):
        for stem in ("dia", "cx", "cy", "cz", "ua", "ub", "d"):
            shapes[stem + name] = full
    shapes["f3"] = full3
    shapes["r0"], shapes["r1"] = (x0, y0 + 8, z0), (x1, y1 + 8, z1)
    shapes["ab2"] = shapes["f2"] = (X2, Y2, LANES)
    for stem in ("ab2", "f2"):
        shapes[stem + "_src"] = shapes[stem + "_junk"] = (x2, y2, LANES)
    shapes["top"] = shapes["top_junk"] = (8, LANES)
    shapes["tops"] = (n, 8, LANES)
    scratch = {name: pltpu.VMEM(shape, jnp.float32) for name, shape in shapes.items()}
    scratch["halo_send"] = pltpu.SemaphoreType.DMA((6, 8))
    scratch["halo_recv"] = pltpu.SemaphoreType.DMA((6, 8))
    scratch["all_send"] = pltpu.SemaphoreType.DMA((3,))
    scratch["all_recv"] = pltpu.SemaphoreType.DMA((3,))
    return pl.pallas_call(
        functools.partial(kernel, peers, dims),
        out_shape=jax.ShapeDtypeStruct(rhs_field.shape, jnp.float32),
        in_specs=[pl.BlockSpec(memory_space=pltpu.VMEM)] * 3,
        out_specs=pl.BlockSpec(memory_space=pltpu.VMEM),
        scratch_shapes=[scratch],
        compiler_params=pltpu.CompilerParams(
            collective_id=0, has_side_effects=True, vmem_limit_bytes=62 * 2**20),
    )(rhs_field, alpha_coef, beta_coef)


def solution(mesh):
    peers = (mesh.shape["gx"], mesh.shape["gy"])
    spec = P("gx", "gy", None)
    return jax.shard_map(functools.partial(local, peers), mesh=mesh, in_specs=(spec,) * 3,
                         out_specs=spec, check_vma=False)
```

time: 577 us -> 58 us (0.10)
  the two profiles are of different devices: /device:TPU:28 before, /device:TPU:1 now
where the time goes in v1:
time: 58 us; the launch traced here: 57.8 us
  Pallas kernels  56.1 us (97%)
  local copies, waits for them, and re-layouts  1.67 us (3%)
    pallas_call x1, Pallas kernels, local(): pl.pallas_call(functools.partial(kernel, peers, dims), out_shape=jax.Shap...  56.1 us
    unnamed x1, local copies, waits for them, and re-layouts  1.67 us

profile of v1, /device:TPU:1, one launch (start us, length us, event | category | flops | bytes accessed | tf_op | source)
XLA Modules:
  0.0 57.8 jit_solution(1966066434811706529)
XLA Ops:
  0.0 56.1 %shard_map.37 = f32[8,32,256]{2,1,0:T(8,128)} custom-call(f32[8,32,256]{2,1,0:T(8,128)} %rhs.1, f32[8,32,256]{2,1,0:T(8,128)} %alpha.1, f32[8,32,256]{2,1,0:T(8,128)} %beta.1), custom_call_target="tpu_custom_call" | custom-call | tf_op jit(solution)/shard_map/pallas_call | solution.py:470
  56.1 1.7 %copy.5 = f32[8,32,256]{2,1,0:T(8,128)} copy(f32[8,32,256]{2,1,0:T(8,128)} %shard_map.37) | data formatting | bytes 524288

commit v2 on v1

--- a/solution.py
+++ b/solution.py
@@ -46,8 +46,8 @@
 
 
 class Exchange:
-    def __init__(self, buf, st_next, st_prev, sems, slot, x_len, y_len, place, peers):
-        self.buf, self.st_next, self.st_prev = buf, st_next, st_prev
+    def __init__(self, buf, sems, slot, x_len, y_len, place, peers):
+        self.buf = buf
         self.send, self.recv = sems
         self.slot, self.x_len, self.y_len = slot, x_len, y_len
         self.place, self.peers = place, peers
@@ -63,9 +63,8 @@
         if dy == 0:
             return (self.buf.at[:, src_x, pl.ds(0, y_len)],
                     self.buf.at[:, dst_x, pl.ds(0, y_len)])
-        if dy == 1:
-            return self.buf.at[:, src_x, pl.ds(y_len - 8, 8)], self.st_prev.at[:, dst_x]
-        return self.buf.at[:, src_x, pl.ds(0, 8)], self.st_next.at[:, dst_x]
+        src_y, dst_y = (y_len - 4, y_len + 4) if dy == 1 else (0, y_len)
+        return self.buf.at[:, src_x, pl.ds(src_y, 4)], self.buf.at[:, dst_x, pl.ds(dst_y, 4)]
 
     def inside(self, dx, dy):
         x, y = self.place[0] + dx, self.place[1] + dy
@@ -101,9 +100,6 @@
             @pl.when(self.inside(-dx, -dy))
             def _():
                 self.copy(k).wait_recv()
-        shape = self.st_next.shape
-        near = iota(shape, 2) < 4
-        self.buf[:, :, pl.ds(self.y_len, 8)] = jnp.where(near, self.st_next[...], self.st_prev[...])
 
 
 def over(start, count, chunk, body):
@@ -111,11 +107,18 @@
         body(start)
         return
 
+    times = count // chunk
+    group = max(k for k in range(1, 6) if times % k == 0)
+
     def step(i, carry):
-        body(start + i * chunk)
+        for k in range(group):
+            body(start + (i * group + k) * chunk)
         return carry
 
-    lax.fori_loop(0, count // chunk, step, 0)
+    if times == group:
+        step(0, 0)
+    else:
+        lax.fori_loop(0, times // group, step, 0)
 
 
 def build(level, start, count, chunk, alpha_at, beta_at, z_len, wrap_y, coefs):
@@ -221,7 +224,7 @@
     lax.fori_loop(1, n, greet, 0)
 
     def exchange(name, slot, x_len, y_len):
-        return Exchange(sc[name], sc[name + "_n"], sc[name + "_p"], sems, slot, x_len, y_len,
+        return Exchange(sc[name], sems, slot, x_len, y_len,
                         place, peers)
 
     ex_in = exchange("in0", 0, x0, y0)
@@ -249,8 +252,8 @@
         pltpu.make_async_copy(whole, whole, sc["all_recv"].at[slot]).wait()
         pltpu.make_async_copy(whole, whole, sc["all_send"].at[slot]).wait()
 
-    def mine(ref):
-        return ref.at[pl.ds(g_x * x2, x2), pl.ds(pl.multiple_of(g_y * y2, y2), y2)]
+    def mine(ref, planes):
+        return ref.at[pl.ds(g_x * planes, planes), pl.ds(pl.multiple_of(g_y * y2, y2), y2)]
 
     in0 = sc["in0"]
     for k, ref in enumerate((rhs, alpha, beta)):
@@ -259,10 +262,10 @@
     ex_in.start()
 
     a1, b1 = restrict_sum(alpha[...], LANES), restrict_sum(beta[...], LANES)
-    row = iota((8, LANES), 0)
-    tile = jnp.where(row == 0, jnp.max(alpha[...]), 0.0)
+    kind = iota((1, LANES), 1) >> 5
+    tile = jnp.full((1, LANES), jnp.max(alpha[...]))
     for k, value in ((1, jnp.max(beta[...])), (2, jnp.max(a1)), (3, jnp.max(b1))):
-        tile = jnp.where(row == k, value, tile)
+        tile = jnp.where(kind == k, value, tile)
     sc["top"][...] = tile
     gather_start(0, sc["top"], lambda: sc["tops"].at[me], sc["top_junk"])
     ab1 = sc["ab1"]
@@ -270,7 +273,7 @@
     ab1[1, pl.ds(HALO, x1), pl.ds(0, y1)] = b1
     ex_ab.start()
     sc["ab2_src"][...] = restrict_sum(a1, LANES) + roll(restrict_sum(b1, LANES), z2, 2)
-    gather_start(1, sc["ab2_src"], lambda: mine(sc["ab2"]), sc["ab2_junk"])
+    gather_start(1, sc["ab2_src"], lambda: mine(sc["ab2"], x2), sc["ab2_junk"])
 
     for ex in (ex_in, ex_ab, ex_f1, ex_u0, ex_u1, ex_v1):
         ex.clear()
@@ -283,9 +286,9 @@
                                0.5 * (in0[2, 0:1] + in0[2, 1:2]), 0.0)
     gather_wait(0, sc["tops"])
     tops = jnp.max(sc["tops"][...], axis=0)
-    wide = jnp.concatenate([tops, tops], axis=1)
-    upper0 = HELM_SHIFT * wide[0:1] + 12.0 * wide[1:2]
-    upper1 = HELM_SHIFT * tops[2:3] + 12.0 * tops[3:4] / 4.0
+    greatest = [jnp.max(jnp.where(kind == k, tops, 0.0), axis=1, keepdims=True) for k in range(4)]
+    upper0 = HELM_SHIFT * greatest[0] + 12.0 * greatest[1] + jnp.zeros((1, z0), jnp.float32)
+    upper1 = HELM_SHIFT * greatest[2] + 12.0 * greatest[3] / 4.0 + jnp.zeros((1, z1), jnp.float32)
     ch0 = cheb(upper0, PRE_STEPS)
     ch1 = cheb(upper1, PRE_STEPS)
     f0 = planes_at(in0, 0, 1)
@@ -311,8 +314,9 @@
     sweep(k1, ua1, ub1, d1, f1, *ch1[1], 1, x1 + 4, 2)
     sweep(k1, ub1, ua1, d1, f1, *ch1[2], 2, x1 + 2, 2)
     residual(k1, ua1, f1, sc["r1"], HALO, x1, 2)
-    sc["f2_src"][...] = restrict_sum(sc["r1"][:, 0:y1], LANES)
-    gather_start(2, sc["f2_src"], lambda: mine(sc["f2"]), sc["f2_junk"])
+    f2_own = restrict_sum(sc["r1"][:, 0:y1], LANES).reshape(x2 // 2, 2, y2, LANES)
+    sc["f2_src"][...] = f2_own[:, 0] + roll(f2_own[:, 1], z2, 2)
+    gather_start(2, sc["f2_src"], lambda: mine(sc["f2_pair"], x2 // 2), sc["f2_junk"])
     sc["u1"][0, pl.ds(HALO, x1), pl.ds(0, y1)] = ua1[pl.ds(HALO, x1), pl.ds(0, y1)]
     ex_u1.start()
 
@@ -353,7 +357,15 @@
 
     ch2 = cheb(HELM_SHIFT * largest(ub2) + 12.0 * largest(d2) / 16.0, PRE_STEPS)
     ch3 = cheb(HELM_SHIFT * largest(ub3) + 12.0 * largest(d3) / 64.0, COARSE_STEPS)
-    gather_wait(2, sc["f2"])
+    gather_wait(2, sc["f2_pair"])
+
+    def unpack_f(i):
+        both = sc["f2_pair"][pl.ds(i, 1)]
+        low = iota(both.shape, 2) < z2
+        sc["f2"][pl.ds(2 * i, 1)] = jnp.where(low, both, 0.0)
+        sc["f2"][pl.ds(2 * i + 1, 1)] = jnp.where(low, roll(both, z2, 2), 0.0)
+
+    over(0, X2 // 2, 1, unpack_f)
     f2 = lambda i: sc["f2"][pl.ds(i - 1, q2)]
     first(ua2, d2, f2, ch2[0][1], 1, X2, q2)
     sweep(k2, ua2, ub2, d2, f2, *ch2[1], 1, X2, q2)
@@ -449,7 +461,6 @@
     shapes = {}
     for name, (k, x, y, z) in wide.items():
         shapes[name] = (k, x + 2 * HALO, y + 8, z)
-        shapes[name + "_n"] = shapes[name + "_p"] = (k, x + 2 * HALO, 8, z)
     full0, full1 = (x0 + 6, y0 + 8, z0), (x1 + 6, y1 + 8, z1)
     full2, full3 = (X2 + 2, Y2, LANES), (X3 + 2, Y3, LANES)
     for name, full in (("0", full0), ("1", full1), ("2", full2), ("3", full3)):
@@ -458,10 +469,11 @@
     shapes["f3"] = full3
     shapes["r0"], shapes["r1"] = (x0, y0 + 8, z0), (x1, y1 + 8, z1)
     shapes["ab2"] = shapes["f2"] = (X2, Y2, LANES)
-    for stem in ("ab2", "f2"):
-        shapes[stem + "_src"] = shapes[stem + "_junk"] = (x2, y2, LANES)
-    shapes["top"] = shapes["top_junk"] = (8, LANES)
-    shapes["tops"] = (n, 8, LANES)
+    shapes["f2_pair"] = (X2 // 2, Y2, LANES)
+    shapes["ab2_src"] = shapes["ab2_junk"] = (x2, y2, LANES)
+    shapes["f2_src"] = shapes["f2_junk"] = (x2 // 2, y2, LANES)
+    shapes["top"] = shapes["top_junk"] = (1, LANES)
+    shapes["tops"] = (n, 1, LANES)
     scratch = {name: pltpu.VMEM(shape, jnp.float32) for name, shape in shapes.items()}
     scratch["halo_send"] = pltpu.SemaphoreType.DMA((6, 8))
     scratch["halo_recv"] = pltpu.SemaphoreType.DMA((6, 8))

time: 58 us -> 47.1 us (0.81)
  Pallas kernels: 56.1 us -> 45.2 us
    pallas_call x1, Pallas kernels: 56.1 us -> 45.2 us  [local(): pl.pallas_call(functools.partial(kernel, peers, dims), out_shape=jax.Shap...]
where the time goes in v2:
time: 47.1 us; the launch traced here: 46.9 us
  Pallas kernels  45.2 us (96%)
  local copies, waits for them, and re-layouts  1.67 us (4%)
    pallas_call x1, Pallas kernels, local(): pl.pallas_call(functools.partial(kernel, peers, dims), out_shape=jax.Shap...  45.2 us
    unnamed x1, local copies, waits for them, and re-layouts  1.67 us

profile of v2, /device:TPU:1, one launch (start us, length us, event | category | flops | bytes accessed | tf_op | source)
XLA Modules:
  0.0 46.9 jit_solution(8622410218398720821)
XLA Ops:
  0.0 45.2 %shard_map.37 = f32[8,32,256]{2,1,0:T(8,128)} custom-call(f32[8,32,256]{2,1,0:T(8,128)} %rhs.1, f32[8,32,256]{2,1,0:T(8,128)} %alpha.1, f32[8,32,256]{2,1,0:T(8,128)} %beta.1), custom_call_target="tpu_custom_call" | custom-call | tf_op jit(solution)/shard_map/pallas_call | solution.py:482
  45.2 1.7 %copy.5 = f32[8,32,256]{2,1,0:T(8,128)} copy(f32[8,32,256]{2,1,0:T(8,128)} %shard_map.37) | data formatting | bytes 524288

commit v3 on v2

--- a/solution.py
+++ b/solution.py
@@ -156,14 +156,14 @@
 
 
 def cheb(upper, steps):
-    lower = LOW_FRACTION * upper
-    middle, half = 0.5 * (upper + lower), 0.5 * (upper - lower)
+    middle, half = 0.5 * (1.0 + LOW_FRACTION), 0.5 * (1.0 - LOW_FRACTION)
     scaled = middle / half
     factor = 1.0 / scaled
-    out = [(None, 1.0 / middle)]
+    inverse = 1.0 / upper
+    out = [(None, inverse * (1.0 / middle))]
     for _ in range(1, steps):
         new = 1.0 / (2.0 * scaled - factor)
-        out.append((new * factor, 2.0 * new / half))
+        out.append((new * factor, inverse * (2.0 * new / half)))
         factor = new
     return out
 
@@ -205,23 +205,48 @@
 
 def kernel(peers, dims, rhs, alpha, beta, out, sc):
     n_x, n_y = peers
-    n = n_x * n_y
     g_x, g_y = lax.axis_index("gx"), lax.axis_index("gy")
     place = (g_x, g_y)
-    me = g_x * n_y + g_y
     (x0, y0, z0), (x1, y1, z1), (x2, y2, z2), (x3, y3, z3) = dims
     X2, Y2, X3, Y3 = n_x * x2, n_y * y2, n_x * x3, n_y * y3
     sems = (sc["halo_send"], sc["halo_recv"])
 
     barrier = pltpu.get_barrier_semaphore()
 
-    def greet(t, carry):
-        j = lax.rem(me + t, n)
-        pl.semaphore_signal(barrier, inc=1, device_id=(lax.div(j, n_y), lax.rem(j, n_y)),
-                            device_id_type=MESH)
-        return carry
-
-    lax.fori_loop(1, n, greet, 0)
+    def each(count, body):
+        if count <= 8:
+            for t in range(1, count):
+                body(t)
+        else:
+            def step(t, carry):
+                body(t)
+                return carry
+
+            lax.fori_loop(1, count, step, 0)
+
+    along_x = lambda t: (lax.rem(g_x + t, n_x), g_y)
+    along_y = lambda t: (g_x, lax.rem(g_y + t, n_y))
+
+    def greet(device):
+        pl.semaphore_signal(barrier, inc=1, device_id=device, device_id_type=MESH)
+
+    each(n_x, lambda t: greet(along_x(t)))
+    each(n_y, lambda t: greet(along_y(t)))
+    corners = 0
+    for dx, dy in DIRS[4:]:
+        x, y = g_x + dx, g_y + dy
+        there = (x >= 0) & (x < n_x) & (y >= 0) & (y < n_y)
+        corners = corners + there.astype(jnp.int32)
+
+        @pl.when(there)
+        def _():
+            greet((x, y))
+
+    in0 = sc["in0"]
+    loads = [pltpu.make_async_copy(ref, in0.at[k, pl.ds(HALO, x0), pl.ds(0, y0)], sc["load"].at[k])
+             for k, ref in enumerate((rhs, alpha, beta))]
+    for load in loads:
+        load.start()
 
     def exchange(name, slot, x_len, y_len):
         return Exchange(sc[name], sems, slot, x_len, y_len,
@@ -234,49 +259,59 @@
     ex_u1 = exchange("u1", 4, x1, y1)
     ex_v1 = exchange("v1", 5, x1, y1)
 
-    def gather_start(slot, src, dst_of, junk):
-        send, recv = sc["all_send"].at[slot], sc["all_recv"].at[slot]
-
-        def one(t, carry):
-            j = lax.rem(me + t, n)
+    def spread(slot, src, dst, count, where):
+        def one(t):
             pltpu.make_async_remote_copy(
-                src_ref=src, dst_ref=dst_of(), send_sem=send, recv_sem=recv,
-                device_id=(lax.div(j, n_y), lax.rem(j, n_y)), device_id_type=MESH).start()
-            return carry
-
-        lax.fori_loop(1, n, one, 0)
-        pltpu.make_async_copy(src, dst_of(), recv).start()
-        pltpu.make_async_copy(src, junk, send).start()
-
-    def gather_wait(slot, whole):
-        pltpu.make_async_copy(whole, whole, sc["all_recv"].at[slot]).wait()
-        pltpu.make_async_copy(whole, whole, sc["all_send"].at[slot]).wait()
-
-    def mine(ref, planes):
-        return ref.at[pl.ds(g_x * planes, planes), pl.ds(pl.multiple_of(g_y * y2, y2), y2)]
-
-    in0 = sc["in0"]
-    for k, ref in enumerate((rhs, alpha, beta)):
-        in0[k, pl.ds(HALO, x0), pl.ds(0, y0)] = ref[...]
-    pl.semaphore_wait(barrier, n - 1)
+                src_ref=src, dst_ref=dst, send_sem=sc["all_send"].at[slot],
+                recv_sem=sc["all_recv"].at[slot], device_id=where(t), device_id_type=MESH).start()
+
+        each(count, one)
+
+    def spread_wait(slot, size):
+        pltpu.make_async_copy(size, size, sc["all_recv"].at[slot]).wait()
+        pltpu.make_async_copy(size, size, sc["all_send"].at[slot]).wait()
+
+    def slab(ref, planes):
+        return ref.at[pl.ds(g_x * planes, planes)]
+
+    def gather_y(slot, ref, planes, value):
+        own = ref.at[pl.ds(g_x * planes, planes), pl.ds(pl.multiple_of(g_y * y2, 8), y2)]
+        own[...] = value
+        spread(slot, own, own, n_y, along_y)
+
+    def gather_x(slot, ref, planes):
+        spread_wait(slot, ref.at[pl.ds(0, planes), pl.ds(0, (n_y - 1) * y2)])
+        spread(slot + 1, slab(ref, planes), slab(ref, planes), n_x, along_x)
+
+    def gather_wait(slot, ref, planes):
+        spread_wait(slot + 1, ref.at[pl.ds(0, (n_x - 1) * planes)])
+
+    for ex in (ex_in, ex_ab, ex_f1, ex_u0, ex_u1, ex_v1):
+        ex.clear()
+    for load in loads:
+        load.wait()
+    pl.semaphore_wait(barrier, n_x - 1 + n_y - 1 + corners)
     ex_in.start()
 
-    a1, b1 = restrict_sum(alpha[...], LANES), restrict_sum(beta[...], LANES)
+    a0 = in0[1, pl.ds(HALO, x0), pl.ds(0, y0)]
+    b0 = in0[2, pl.ds(HALO, x0), pl.ds(0, y0)]
+    a1, b1 = restrict_sum(a0, LANES), restrict_sum(b0, LANES)
     kind = iota((1, LANES), 1) >> 5
-    tile = jnp.full((1, LANES), jnp.max(alpha[...]))
-    for k, value in ((1, jnp.max(beta[...])), (2, jnp.max(a1)), (3, jnp.max(b1))):
+    tile = jnp.full((1, LANES), jnp.max(a0))
+    for k, value in ((1, jnp.max(b0)), (2, jnp.max(a1)), (3, jnp.max(b1))):
         tile = jnp.where(kind == k, value, tile)
-    sc["top"][...] = tile
-    gather_start(0, sc["top"], lambda: sc["tops"].at[me], sc["top_junk"])
+    top_y, top_x = sc["top_y"], sc["top_x"]
+    top_y[g_y] = tile
+    spread(0, top_y.at[g_y], top_y.at[g_y], n_y, along_y)
     ab1 = sc["ab1"]
     ab1[0, pl.ds(HALO, x1), pl.ds(0, y1)] = a1
     ab1[1, pl.ds(HALO, x1), pl.ds(0, y1)] = b1
     ex_ab.start()
-    sc["ab2_src"][...] = restrict_sum(a1, LANES) + roll(restrict_sum(b1, LANES), z2, 2)
-    gather_start(1, sc["ab2_src"], lambda: mine(sc["ab2"], x2), sc["ab2_junk"])
-
-    for ex in (ex_in, ex_ab, ex_f1, ex_u0, ex_u1, ex_v1):
-        ex.clear()
+    both2 = restrict_sum(a1, LANES) + roll(restrict_sum(b1, LANES), z2, 2)
+    gather_y(2, sc["ab2"], x2, both2)
+    spread_wait(0, top_y.at[pl.ds(0, n_y - 1)])
+    top_x[g_x] = jnp.max(top_y[...], axis=0)
+    spread(1, top_x.at[g_x], top_x.at[g_x], n_x, along_x)
 
     ex_in.finish()
     k0 = [sc[k] for k in ("dia0", "cx0", "cy0", "cz0")]
@@ -284,8 +319,9 @@
     build(0, 1, x0 + 4, 1, planes_at(in0, 1, 1), planes_at(in0, 2, 1), z0, True, k0)
     sc["cx0"][0:1] = jnp.where(jnp.minimum(in0[2, 0:1], in0[2, 1:2]) > 0.0,
                                0.5 * (in0[2, 0:1] + in0[2, 1:2]), 0.0)
-    gather_wait(0, sc["tops"])
-    tops = jnp.max(sc["tops"][...], axis=0)
+    gather_x(2, sc["ab2"], x2)
+    spread_wait(1, top_x.at[pl.ds(0, n_x - 1)])
+    tops = jnp.max(top_x[...], axis=0)
     greatest = [jnp.max(jnp.where(kind == k, tops, 0.0), axis=1, keepdims=True) for k in range(4)]
     upper0 = HELM_SHIFT * greatest[0] + 12.0 * greatest[1] + jnp.zeros((1, z0), jnp.float32)
     upper1 = HELM_SHIFT * greatest[2] + 12.0 * greatest[3] / 4.0 + jnp.zeros((1, z1), jnp.float32)
@@ -315,8 +351,7 @@
     sweep(k1, ub1, ua1, d1, f1, *ch1[2], 2, x1 + 2, 2)
     residual(k1, ua1, f1, sc["r1"], HALO, x1, 2)
     f2_own = restrict_sum(sc["r1"][:, 0:y1], LANES).reshape(x2 // 2, 2, y2, LANES)
-    sc["f2_src"][...] = f2_own[:, 0] + roll(f2_own[:, 1], z2, 2)
-    gather_start(2, sc["f2_src"], lambda: mine(sc["f2_pair"], x2 // 2), sc["f2_junk"])
+    gather_y(4, sc["f2_pair"], x2 // 2, f2_own[:, 0] + roll(f2_own[:, 1], z2, 2))
     sc["u1"][0, pl.ds(HALO, x1), pl.ds(0, y1)] = ua1[pl.ds(HALO, x1), pl.ds(0, y1)]
     ex_u1.start()
 
@@ -328,7 +363,8 @@
                       (ua3, X3), (ub3, X3), (sc["cx3"], X3), (d3, X3)):
         for at in (0, size + 1):
             ref[at] = jnp.zeros(ref.shape[1:], jnp.float32)
-    gather_wait(1, sc["ab2"])
+    gather_wait(2, sc["ab2"], x2)
+    gather_x(4, sc["f2_pair"], x2 // 2)
     q2 = 2 if X2 % 2 == 0 else 1
     q3 = X3 if X3 * Y3 <= 256 else 1
     fine = max(1, 256 // Y2) * 2
@@ -357,7 +393,7 @@
 
     ch2 = cheb(HELM_SHIFT * largest(ub2) + 12.0 * largest(d2) / 16.0, PRE_STEPS)
     ch3 = cheb(HELM_SHIFT * largest(ub3) + 12.0 * largest(d3) / 64.0, COARSE_STEPS)
-    gather_wait(2, sc["f2_pair"])
+    gather_wait(4, sc["f2_pair"], x2 // 2)
 
     def unpack_f(i):
         both = sc["f2_pair"][pl.ds(i, 1)]
@@ -451,7 +487,6 @@
 
 def local(peers, rhs_field, alpha_coef, beta_coef):
     n_x, n_y = peers
-    n = n_x * n_y
     x0, y0, z0 = rhs_field.shape
     dims = [(x0 >> k, y0 >> k, z0 >> k) for k in range(4)]
     (x0, y0, z0), (x1, y1, z1), (x2, y2, z2), (x3, y3, z3) = dims
@@ -470,19 +505,17 @@
     shapes["r0"], shapes["r1"] = (x0, y0 + 8, z0), (x1, y1 + 8, z1)
     shapes["ab2"] = shapes["f2"] = (X2, Y2, LANES)
     shapes["f2_pair"] = (X2 // 2, Y2, LANES)
-    shapes["ab2_src"] = shapes["ab2_junk"] = (x2, y2, LANES)
-    shapes["f2_src"] = shapes["f2_junk"] = (x2 // 2, y2, LANES)
-    shapes["top"] = shapes["top_junk"] = (1, LANES)
-    shapes["tops"] = (n, 1, LANES)
+    shapes["top_y"], shapes["top_x"] = (n_y, 1, LANES), (n_x, 1, LANES)
     scratch = {name: pltpu.VMEM(shape, jnp.float32) for name, shape in shapes.items()}
     scratch["halo_send"] = pltpu.SemaphoreType.DMA((6, 8))
     scratch["halo_recv"] = pltpu.SemaphoreType.DMA((6, 8))
-    scratch["all_send"] = pltpu.SemaphoreType.DMA((3,))
-    scratch["all_recv"] = pltpu.SemaphoreType.DMA((3,))
+    scratch["all_send"] = pltpu.SemaphoreType.DMA((6,))
+    scratch["all_recv"] = pltpu.SemaphoreType.DMA((6,))
+    scratch["load"] = pltpu.SemaphoreType.DMA((3,))
     return pl.pallas_call(
         functools.partial(kernel, peers, dims),
         out_shape=jax.ShapeDtypeStruct(rhs_field.shape, jnp.float32),
-        in_specs=[pl.BlockSpec(memory_space=pltpu.VMEM)] * 3,
+        in_specs=[pl.BlockSpec(memory_space=pl.ANY)] * 3,
         out_specs=pl.BlockSpec(memory_space=pltpu.VMEM),
         scratch_shapes=[scratch],
         compiler_params=pltpu.CompilerParams(

time: 47.1 us -> 44.7 us (0.949)
  Pallas kernels: 45.2 us -> 42.8 us
    pallas_call x1, Pallas kernels: 45.2 us -> 42.8 us  [local(): pl.pallas_call(functools.partial(kernel, peers, dims), out_shape=jax.Shap...]
where the time goes in v3:
time: 44.7 us; the launch traced here: 44.5 us
  Pallas kernels  42.8 us (96%)
  local copies, waits for them, and re-layouts  1.67 us (4%)
    pallas_call x1, Pallas kernels, local(): pl.pallas_call(functools.partial(kernel, peers, dims), out_shape=jax.Shap...  42.8 us
    unnamed x1, local copies, waits for them, and re-layouts  1.67 us

profile of v3, /device:TPU:1, one launch (start us, length us, event | category | flops | bytes accessed | tf_op | source)
XLA Modules:
  0.0 44.5 jit_solution(6533589540300714383)
XLA Ops:
  0.0 42.8 %shard_map.37 = f32[8,32,256]{2,1,0:T(8,128)} custom-call(f32[8,32,256]{2,1,0:T(8,128)} %rhs.1, f32[8,32,256]{2,1,0:T(8,128)} %alpha.1, f32[8,32,256]{2,1,0:T(8,128)} %beta.1), custom_call_target="tpu_custom_call" | custom-call | tf_op jit(solution)/shard_map/pallas_call | solution.py:515
  42.8 1.7 %copy.5 = f32[8,32,256]{2,1,0:T(8,128)} copy(f32[8,32,256]{2,1,0:T(8,128)} %shard_map.37) | data formatting | bytes 524288

commit v4 on v3

--- a/solution.py
+++ b/solution.py
@@ -16,11 +16,17 @@
 HALO = 3
 MESH = pl.DeviceIdType.MESH
 DIRS = [(1, 0), (-1, 0), (0, 1), (0, -1), (1, 1), (1, -1), (-1, 1), (-1, -1)]
-HIGH = lax.Precision.HIGHEST
 
 
 def dot(a, b):
-    return jnp.dot(a, b, precision=HIGH, preferred_element_type=jnp.float32)
+    total, rest = None, b if a.dtype == jnp.bfloat16 else a
+    for _ in range(3):
+        part = rest.astype(jnp.bfloat16)
+        rest = rest - part.astype(jnp.float32)
+        pair = (a, part) if a.dtype == jnp.bfloat16 else (part, b)
+        term = jnp.dot(*pair, preferred_element_type=jnp.float32)
+        total = term if total is None else total + term
+    return total
 
 
 def iota(shape, dim):
@@ -28,7 +34,7 @@
 
 
 def pick(rows, cols, cond):
-    return cond(iota((rows, cols), 0), iota((rows, cols), 1)).astype(jnp.float32)
+    return cond(iota((rows, cols), 0), iota((rows, cols), 1)).astype(jnp.float32).astype(jnp.bfloat16)
 
 
 def roll(x, shift, axis):

time: 44.7 us -> 43.5 us (0.973)
  Pallas kernels: 42.8 us -> 41.7 us
    pallas_call x1, Pallas kernels: 42.8 us -> 41.7 us  [local(): pl.pallas_call(functools.partial(kernel, peers, dims), out_shape=jax.Shap...]
where the time goes in v4:
time: 43.5 us; the launch traced here: 43.4 us
  Pallas kernels  41.7 us (96%)
  local copies, waits for them, and re-layouts  1.67 us (4%)
    pallas_call x1, Pallas kernels, local(): pl.pallas_call(functools.partial(kernel, peers, dims), out_shape=jax.Shap...  41.7 us
    unnamed x1, local copies, waits for them, and re-layouts  1.67 us

profile of v4, /device:TPU:1, one launch (start us, length us, event | category | flops | bytes accessed | tf_op | source)
XLA Modules:
  0.0 43.4 jit_solution(9492456214139875384)
XLA Ops:
  0.0 41.7 %shard_map.37 = f32[8,32,256]{2,1,0:T(8,128)} custom-call(f32[8,32,256]{2,1,0:T(8,128)} %rhs.1, f32[8,32,256]{2,1,0:T(8,128)} %alpha.1, f32[8,32,256]{2,1,0:T(8,128)} %beta.1), custom_call_target="tpu_custom_call" | custom-call | tf_op jit(solution)/shard_map/pallas_call | solution.py:521
  41.7 1.7 %copy.5 = f32[8,32,256]{2,1,0:T(8,128)} copy(f32[8,32,256]{2,1,0:T(8,128)} %shard_map.37) | data formatting | bytes 524288
